TPU v7x, 32 devices: a whole 2x2x4 slice. The times are simulated.
32 devices in a mesh: grp: 2 (over y), gx: 4 (over z), gy: 2 (over x), gz: 2 (over core).
Axes of the slice: x: 2, y: 2, z: 4, core: 2. Of those that a mesh axis runs over, the one named last changes fastest.
Arguments:
- ensemble: bfloat16 [128, 32, 32, 256], P(('grp', 'gx'), 'gy', 'gz'), parts along dimension 0, may hold values from -40 to 40
- wind_field: float32 [3, 128, 32, 32], P(None, ('grp', 'gx'), 'gy', 'gz'), parts along dimension 1, may hold values from -0.5 to 0.5
- obs_value: float32 [128, 32, 16], P(('grp', 'gx'), 'gy', 'gz'), parts along dimension 0, may hold values from -60 to 60
- obs_weight: float32 [128, 32, 16], P(('grp', 'gx'), 'gy', 'gz'), parts along dimension 0, may hold values from 0.1 to 1.75
- obs_cell: int32 [128, 32, 16], P(('grp', 'gx'), 'gy', 'gz'), parts along dimension 0, may hold values from 0 to 4095, as said below
- obs_used: int32 [128, 32, 16], P(('grp', 'gx'), 'gy', 'gz'), parts along dimension 0, may hold values 0 or 1
Outputs:
- analysis: bfloat16 [128, 32, 32, 256], P(('grp', 'gx'), 'gy', 'gz'), parts along dimension 0
There are 2 independent parts, one for each index of `grp`. A program takes and returns all parts, laid end to end along the dimension named above; each array names one. Nothing has to cross between parts.
Inputs may be any that keep to these rules, and one draw needn't show every extreme that they name: `obs_cell`: each entry names a cell of the grid block held by the same device, numbered (x * 16 + y) * 16 + z inside the block.
All inputs are finite; a program needn't handle non-finite values. No bound on the sum of `obs_used` on one device may be relied on, other than what follows from the above.
Results may differ from a plain program's by a relative error of at most 0.0067.
Values may be sent and summed in bfloat16 or wider, within the bound.
A program may use at most 64 MiB of HBM per device.

v0:
```python
import math
import jax
import jax.numpy as jnp
from jax import lax
from jax.sharding import PartitionSpec as P

ITERS = 5
diffusion = 0.1
steepen = 0.1


def padded_2(block, sides, width):
    for axis, dim in sides:
        count = lax.axis_size(axis)
        forward = [(i, i + 1) for i in range(count - 1)]
        backward = [(target, source) for source, target in forward]
        low = lax.ppermute(
            lax.slice_in_dim(block, block.shape[dim] - width, None, axis=dim), axis, forward
        )
        high = lax.ppermute(lax.slice_in_dim(block, 0, width, axis=dim), axis, backward)
        block = jnp.concatenate([low, block, high], axis=dim)
    return block


def advance(padded, wind_field):
    centre = padded[1:-1, 1:-1, 1:-1].astype(jnp.float32)
    ahead_x = padded[2:, 1:-1, 1:-1].astype(jnp.float32)
    behind_x = padded[:-2, 1:-1, 1:-1].astype(jnp.float32)
    ahead_y = padded[1:-1, 2:, 1:-1].astype(jnp.float32)
    behind_y = padded[1:-1, :-2, 1:-1].astype(jnp.float32)
    ahead_z = padded[1:-1, 1:-1, 2:].astype(jnp.float32)
    behind_z = padded[1:-1, 1:-1, :-2].astype(jnp.float32)
    laplace = ahead_x + behind_x + ahead_y + behind_y + ahead_z + behind_z - 6.0 * centre
    transport = (wind_field[0][..., None] + steepen * centre) * (ahead_x - behind_x)
    transport = transport + wind_field[1][..., None] * (ahead_y - behind_y)
    transport = transport + wind_field[2][..., None] * (ahead_z - behind_z)
    return lax.optimization_barrier(
        (centre + diffusion * laplace - 0.5 * transport).astype(jnp.bfloat16)
    )


def product(left, right):
    return jnp.dot(left, right, precision=lax.Precision.HIGHEST)


def inverse_root(gram_full):
    member_states = gram_full.shape[0]
    identity = jnp.eye(member_states, dtype=jnp.float32)
    coupled = identity + gram_full
    frob_norm = jnp.sqrt(jnp.sum(coupled * coupled))
    iterate_y = coupled / frob_norm
    iterate_z = identity
    for sweep in range(ITERS):
        factor_p = 0.5 * (3.0 * identity - product(iterate_z, iterate_y))
        iterate_y = product(factor_p, iterate_y)
        iterate_z = product(factor_p, iterate_z)
    return iterate_z / jnp.sqrt(frob_norm)


def per_device(ensemble, wind_field, obs_value, obs_weight, obs_cell, obs_used):
    extent_x, extent_y, extent_z, member_states = ensemble.shape

    def advance_border(field):
        padded = padded_2(field, (("gx", 0), ("gy", 1), ("gz", 2)), 1)
        return advance(padded, wind_field)

    predicted_state = advance_border(advance_border(ensemble))
    ensemble_average = jnp.mean(predicted_state.astype(jnp.float32), axis=3)
    member_departures = (predicted_state.astype(jnp.float32) - ensemble_average[..., None]).astype(
        jnp.bfloat16
    )
    flat_anom = member_departures.reshape(-1, member_states)
    mean_flat = ensemble_average.reshape(-1)
    obs_spots = obs_cell.reshape(-1)
    picked = jnp.take(flat_anom, obs_spots, axis=0)
    mean_at = jnp.take(mean_flat, obs_spots, axis=0)
    obs_total = obs_cell.size * lax.axis_size("gx") * lax.axis_size("gy") * lax.axis_size("gz")
    in_use = obs_used.reshape(-1).astype(jnp.float32)
    obs_scale = obs_weight.reshape(-1)
    values = obs_value.reshape(-1)
    scaled = (
        (in_use * obs_scale / math.sqrt(obs_total))[:, None] * picked.astype(jnp.float32)
    ).astype(jnp.bfloat16)
    innovation = (in_use * obs_scale * (values - mean_at) / math.sqrt(obs_total)).astype(
        jnp.bfloat16
    )
    gram_part = lax.dot_general(
        scaled, scaled, (((0,), (0,)), ((), ())), preferred_element_type=jnp.float32
    )
    couple_part = jnp.dot(innovation, scaled, preferred_element_type=jnp.float32)
    gram_full, coupling = lax.psum((gram_part, couple_part), ("gx", "gy", "gz"))
    transform = inverse_root(gram_full)
    shift = product(transform, product(transform, coupling))
    weights = (transform + shift[:, None]).astype(jnp.bfloat16)
    mixed = jnp.dot(flat_anom, weights, preferred_element_type=jnp.float32)
    analysis = (mean_flat[:, None] + mixed).astype(jnp.bfloat16)
    return analysis.reshape(extent_x, extent_y, extent_z, member_states)


def solution(mesh):
    in_specs = (
        P(("grp", "gx"), "gy", "gz", None),
        P(None, ("grp", "gx"), "gy", "gz"),
        P(("grp", "gx"), "gy", "gz"),
        P(("grp", "gx"), "gy", "gz"),
        P(("grp", "gx"), "gy", "gz"),
        P(("grp", "gx"), "gy", "gz"),
    )
    out_specs = P(("grp", "gx"), "gy", "gz", None)
    return jax.shard_map(
        per_device, mesh=mesh, in_specs=in_specs, out_specs=out_specs, check_vma=False
    )
```

profile of v0, /device:TPU:1, one launch (start us, length us, event | category | flops | bytes accessed | tf_op | source)
XLA Modules:
  0.0 221.4 jit_solution(8572135581183431103)
XLA Ops:
  6.5 1.0 fusion.37
  7.5 4.0 %collective-permute-start.1 = (bf16[1,16,16,256]{3,2,1,0:T(8,128)(2,1)S(1)}, bf16[1,16,16,256]{3,2,1,0:T(8,128)(2,1)S(1)}, u32[]{:S(2)}, u32[]{:S(2)}) collective-permute-start(bf16[1,16,16,256]{3,2,1,0:T(8,128)(2,1)S(1)} %get-tuple-element.18), channel_id=1, source_target_pairs={{0,4},{4,8},{8,12},{1,5},{5,9},{9,13},{2,6},{6,10},{10,14},{3,7},{... | collective-permute-start | bytes 393224 | tf_op jit(solution)/shard_map/ppermute | solution.py:17
  11.6 1.3 collective-permute-start
  12.9 0.8 collective-permute-done.1
  13.7 1.8 constant_dynamic-update-slice_fusion.1
  15.6 1.7 collective-permute-done
  17.3 1.3 collective-permute-start.2
  18.6 4.0 %collective-permute-start.3 = (bf16[18,1,16,256]{3,2,1,0:T(8,128)(2,1)S(1)}, bf16[18,1,16,256]{3,2,1,0:T(8,128)(2,1)S(1)}, u32[]{:S(2)}, u32[]{:S(2)}) collective-permute-start(bf16[18,1,16,256]{3,2,1,0:T(8,128)(2,1)S(1)} %get-tuple-element.13), channel_id=1, source_target_pairs={{0,2},{1,3},{4,6},{5,7},{8,10},{9,11},{12,14},{13,15},{16,18},{17,... | collective-permute-start | bytes 442376 | tf_op jit(solution)/shard_map/ppermute | solution.py:17
  23.2 1.5 collective-permute-done.3
  24.7 0.5 pad_maximum_fusion.35
  25.3 5.2 %collective-permute-start.4 = (bf16[18,18,1,256]{3,1,2,0:T(8,128)(2,1)S(1)}, bf16[18,18,1,256]{3,1,2,0:T(8,128)(2,1)S(1)}, u32[]{:S(2)}, u32[]{:S(2)}) collective-permute-start(bf16[18,18,1,256]{3,1,2,0:T(8,128)(2,1)S(1)} %copy.40), channel_id=1, source_target_pairs={{1,0},{3,2},{5,4},{7,6},{9,8},{11,10},{13,12},{15,14},{17,16},{19,... | collective-permute-start | bytes 497672 | tf_op jit(solution)/shard_map/ppermute | solution.py:20
  30.5 1.4 collective-permute-start.5
  32.0 1.1 slice_bitcast_fusion.2
  33.3 0.7 collective-permute-done.5
  34.3 10.0 %fusion.6 = bf16[16,16,16,256]{3,2,1,0:T(8,128)(2,1)S(1)} fusion(bf16[16,16,16,256]{3,2,1,0:T(8,128)(2,1)S(1)} %copy-done.3, bf16[18,18,1,256]{3,2,1,0:T(2,128)(2,1)S(1)} %copy.43, bf16[18,1,16,256]{3,2,1,0:T(8,128)(2,1)S(1)} %collective-permute-done.2, bf16[18,16,16,256]{3,2,1,0:T(8,128)(2,1)S(1)} %copy-done.2, ...), kind=kLoop, calls=%fused_computation.33 | loop fusion | flops 57671680 | bytes 7491584 | tf_op jit(solution)/shard_map/convert_element_type | solution.py:38
  44.3 1.3 collective-permute-start.6
  45.6 4.0 %collective-permute-start.7 = (bf16[1,16,16,256]{3,2,1,0:T(8,128)(2,1)S(1)}, bf16[1,16,16,256]{3,2,1,0:T(8,128)(2,1)S(1)}, u32[]{:S(2)}, u32[]{:S(2)}) collective-permute-start(bf16[1,16,16,256]{3,2,1,0:T(8,128)(2,1)S(1)} %get-tuple-element.15), channel_id=1, source_target_pairs={{0,4},{4,8},{8,12},{1,5},{5,9},{9,13},{2,6},{6,10},{10,14},{3,7},{... | collective-permute-start | bytes 393224 | tf_op jit(solution)/shard_map/ppermute | solution.py:17
  49.7 1.1 collective-permute-done.6
  50.9 0.9 collective-permute-done.7
  51.8 1.3 collective-permute-start.8
  53.1 4.1 %collective-permute-start.9 = (bf16[18,1,16,256]{3,2,1,0:T(8,128)(2,1)S(1)}, bf16[18,1,16,256]{3,2,1,0:T(8,128)(2,1)S(1)}, u32[]{:S(2)}, u32[]{:S(2)}) collective-permute-start(bf16[18,1,16,256]{3,2,1,0:T(8,128)(2,1)S(1)} %get-tuple-element.11), channel_id=1, source_target_pairs={{0,2},{1,3},{4,6},{5,7},{8,10},{9,11},{12,14},{13,15},{16,18},{17,... | collective-permute-start | bytes 442376 | tf_op jit(solution)/shard_map/ppermute | solution.py:17
  57.2 0.9 convert_multiply_fusion.4
  58.3 0.9 copy.54
  59.3 0.7 pad_maximum_fusion.32
  60.1 4.4 %collective-permute-start.10 = (bf16[18,18,1,256]{3,1,2,0:T(8,128)(2,1)S(1)}, bf16[18,18,1,256]{3,1,2,0:T(8,128)(2,1)S(1)}, u32[]{:S(2)}, u32[]{:S(2)}) collective-permute-start(bf16[18,18,1,256]{3,1,2,0:T(8,128)(2,1)S(1)} %copy.44), channel_id=1, source_target_pairs={{1,0},{3,2},{5,4},{7,6},{9,8},{11,10},{13,12},{15,14},{17,16},{19,... | collective-permute-start | bytes 497672 | tf_op jit(solution)/shard_map/ppermute | solution.py:20
  64.6 1.3 collective-permute-start.11
  66.2 1.8 collective-permute-done.11
  68.2 13.7 %fusion.16 = bf16[16,16,16,256]{3,2,1,0:T(8,128)(2,1)S(1)} fusion(bf16[16,16,16,256]{3,2,1,0:T(8,128)(2,1)S(1)} %fusion.6, bf16[18,18,1,256]{3,2,1,0:T(2,128)(2,1)S(1)} %copy.47, bf16[18,1,16,256]{3,2,1,0:T(8,128)(2,1)S(1)} %collective-permute-done.8, bf16[18,1,16,256]{3,2,1,0:T(8,128)(2,1)S(1)} %collective-permute-done.9, ...), kind=kLoop, calls=%fused_computation.43 | loop fusion | flops 74448896 | bytes 5132288 | tf_op jit(solution)/shard_map/convert_element_type | solution.py:38
  81.9 1.3 copy-done
  83.2 0.6 convert_reduce_fusion
  84.0 1.9 fusion.21
  86.1 9.1 %gather_fusion = bf16[2048,256]{1,0:T(8,128)(2,1)} fusion(bf16[4096,256]{1,0:T(8,128)(2,1)S(1)} %bitcast.48, s32[2048]{0:T(1024)S(1)} %broadcast_clamp_fusion), kind=kCustom, calls=%fused_computation | custom fusion | bytes 2105344 | tf_op jit(solution)/shard_map/jit(_take)/gather | solution.py:75
  95.2 11.8 %gather_fusion.1 = f32[2048]{0:T(1024)S(1)} fusion(f32[4096]{0:T(1024)S(1)} %div.28, s32[2048]{0:T(1024)S(1)} %broadcast_clamp_fusion), kind=kCustom, calls=%fused_computation.1 | custom fusion | bytes 24576 | tf_op jit(solution)/shard_map/jit(_take)/gather | solution.py:76
  107.0 1.8 multiply_convert_fusion
  108.7 1.2 fusion.38
  110.2 31.3 %psum.15 = f32[256]{0:T(256)S(1)} all-reduce(f32[256]{0:T(256)S(1)} %bitcast.53), channel_id=1, replica_groups=mesh['grp'=2,'gx'=4,'gy'=2,'gz'=2] {'gx','gy','gz'}, use_global_device_ids=true, to_apply=%region_3.4 | all-reduce | flops 256 | bytes 2048 | tf_op jit(solution)/shard_map/psum | solution.py:91
  141.5 60.8 %all-reduce.2.cloned.1.call-done = f32[256,256]{1,0:T(8,128)} async-done(((f32[256,256]{1,0:T(8,128)}), f32[256,256]{1,0:T(8,128)}) %all-reduce.2.cloned.1.call-update) | async-done | bytes 262160 | tf_op jit(solution)/shard_map/psum | solution.py:91
  202.3 1.6 multiply_reduce_fusion
  204.6 1.3 fusion.28
  206.2 1.4 fusion.32
  207.5 0.4 fusion.27
  207.9 0.4 fusion.40
  208.7 0.4 fusion.26
  209.5 0.4 fusion.41
  209.9 0.4 fusion.25
  211.1 0.4 fusion.24
  211.5 0.4 convolution_divide_fusion
  212.4 2.1 fusion
  (51 shorter events, 5.2 us)
Async XLA Ops:
  6.5 195.7 %all-reduce.2.cloned.1.call-start = ((), (), s32[]{:S(2)}) async-start(), calls=%async_computation | async-start | bytes 524288 | tf_op jit(solution)/shard_map/psum | solution.py:91
  7.5 6.2 %collective-permute-start.1 = (bf16[1,16,16,256]{3,2,1,0:T(8,128)(2,1)S(1)}, bf16[1,16,16,256]{3,2,1,0:T(8,128)(2,1)S(1)}, u32[]{:S(2)}, u32[]{:S(2)}) collective-permute-start(bf16[1,16,16,256]{3,2,1,0:T(8,128)(2,1)S(1)} %get-tuple-element.18), channel_id=1, source_target_pairs={{0,4},{4,8},{8,12},{1,5},{5,9},{9,13},{2,6},{6,10},{10,14},{3,7},{... | collective-permute-start | bytes 393224 | tf_op jit(solution)/shard_map/ppermute | solution.py:17
  11.6 5.7 %collective-permute-start = (bf16[1,16,16,256]{3,2,1,0:T(8,128)(2,1)S(1)}, bf16[1,16,16,256]{3,2,1,0:T(8,128)(2,1)S(1)}, u32[]{:S(2)}, u32[]{:S(2)}) collective-permute-start(bf16[1,16,16,256]{3,2,1,0:T(8,128)(2,1)S(1)} %get-tuple-element.17), channel_id=1, source_target_pairs={{4,0},{8,4},{12,8},{5,1},{9,5},{13,9},{6,2},{10,6},{14,10},{7,3},{... | collective-permute-start | bytes 393224 | tf_op jit(solution)/shard_map/ppermute | solution.py:20
  13.7 8.9 %copy-start.4 = (s32[16,16,8]{1,2,0:T(8,128)S(1)}, s32[16,16,8]{1,2,0:T(8,128)}, u32[]{:S(2)}) copy-start(s32[16,16,8]{1,2,0:T(8,128)} %param.10) | copy-start | bytes 24580
  17.3 8.0 %copy-start.1 = (bf16[18,16,16,256]{3,2,1,0:T(8,128)(2,1)}, bf16[18,16,16,256]{3,2,1,0:T(8,128)(2,1)S(1)}, u32[]{:S(2)}) copy-start(bf16[18,16,16,256]{3,2,1,0:T(8,128)(2,1)S(1)} %constant_dynamic-update-slice_fusion) | copy-start | bytes 7077892
  17.3 5.9 %collective-permute-start.2 = (bf16[18,1,16,256]{3,2,1,0:T(8,128)(2,1)S(1)}, bf16[18,1,16,256]{3,2,1,0:T(8,128)(2,1)S(1)}, u32[]{:S(2)}, u32[]{:S(2)}) collective-permute-start(bf16[18,1,16,256]{3,2,1,0:T(8,128)(2,1)S(1)} %get-tuple-element.14), channel_id=1, source_target_pairs={{2,0},{3,1},{6,4},{7,5},{10,8},{11,9},{14,12},{15,13},{18,16},{19,... | collective-permute-start | bytes 442376 | tf_op jit(solution)/shard_map/ppermute | solution.py:20
  18.6 6.1 %collective-permute-start.3 = (bf16[18,1,16,256]{3,2,1,0:T(8,128)(2,1)S(1)}, bf16[18,1,16,256]{3,2,1,0:T(8,128)(2,1)S(1)}, u32[]{:S(2)}, u32[]{:S(2)}) collective-permute-start(bf16[18,1,16,256]{3,2,1,0:T(8,128)(2,1)S(1)} %get-tuple-element.13), channel_id=1, source_target_pairs={{0,2},{1,3},{4,6},{5,7},{8,10},{9,11},{12,14},{13,15},{16,18},{17,... | collective-permute-start | bytes 442376 | tf_op jit(solution)/shard_map/ppermute | solution.py:17
  22.9 11.4 %copy-start.3 = (bf16[16,16,16,256]{3,2,1,0:T(8,128)(2,1)S(1)}, bf16[16,16,16,256]{3,2,1,0:T(8,128)(2,1)}, u32[]{:S(2)}) copy-start(bf16[16,16,16,256]{3,2,1,0:T(8,128)(2,1)} %param.6) | copy-start | bytes 6291460
  25.3 7.7 %collective-permute-start.4 = (bf16[18,18,1,256]{3,1,2,0:T(8,128)(2,1)S(1)}, bf16[18,18,1,256]{3,1,2,0:T(8,128)(2,1)S(1)}, u32[]{:S(2)}, u32[]{:S(2)}) collective-permute-start(bf16[18,18,1,256]{3,1,2,0:T(8,128)(2,1)S(1)} %copy.40), channel_id=1, source_target_pairs={{1,0},{3,2},{5,4},{7,6},{9,8},{11,10},{13,12},{15,14},{17,16},{19,... | collective-permute-start | bytes 497672 | tf_op jit(solution)/shard_map/ppermute | solution.py:20
  30.5 3.8 %copy-start.2 = (bf16[18,16,16,256]{3,2,1,0:T(8,128)(2,1)S(1)}, bf16[18,16,16,256]{3,2,1,0:T(8,128)(2,1)}, u32[]{:S(2)}) copy-start(bf16[18,16,16,256]{3,2,1,0:T(8,128)(2,1)} %copy-done.1) | copy-start | bytes 7077892
  30.5 3.5 %collective-permute-start.5 = (bf16[18,18,1,256]{3,1,2,0:T(8,128)(2,1)S(1)}, bf16[18,18,1,256]{3,1,2,0:T(8,128)(2,1)S(1)}, u32[]{:S(2)}, u32[]{:S(2)}) collective-permute-start(bf16[18,18,1,256]{3,1,2,0:T(8,128)(2,1)S(1)} %copy.42), channel_id=1, source_target_pairs={{0,1},{2,3},{4,5},{6,7},{8,9},{10,11},{12,13},{14,15},{16,17},{18,... | collective-permute-start | bytes 497672 | tf_op jit(solution)/shard_map/ppermute | solution.py:17
  44.3 6.5 %collective-permute-start.6 = (bf16[1,16,16,256]{3,2,1,0:T(8,128)(2,1)S(1)}, bf16[1,16,16,256]{3,2,1,0:T(8,128)(2,1)S(1)}, u32[]{:S(2)}, u32[]{:S(2)}) collective-permute-start(bf16[1,16,16,256]{3,2,1,0:T(8,128)(2,1)S(1)} %get-tuple-element.16), channel_id=1, source_target_pairs={{4,0},{8,4},{12,8},{5,1},{9,5},{13,9},{6,2},{10,6},{14,10},{7,3},{... | collective-permute-start | bytes 393224 | tf_op jit(solution)/shard_map/ppermute | solution.py:20
  45.6 6.1 %collective-permute-start.7 = (bf16[1,16,16,256]{3,2,1,0:T(8,128)(2,1)S(1)}, bf16[1,16,16,256]{3,2,1,0:T(8,128)(2,1)S(1)}, u32[]{:S(2)}, u32[]{:S(2)}) collective-permute-start(bf16[1,16,16,256]{3,2,1,0:T(8,128)(2,1)S(1)} %get-tuple-element.15), channel_id=1, source_target_pairs={{0,4},{4,8},{8,12},{1,5},{5,9},{9,13},{2,6},{6,10},{10,14},{3,7},{... | collective-permute-start | bytes 393224 | tf_op jit(solution)/shard_map/ppermute | solution.py:17
  51.8 7.6 %collective-permute-start.8 = (bf16[18,1,16,256]{3,2,1,0:T(8,128)(2,1)S(1)}, bf16[18,1,16,256]{3,2,1,0:T(8,128)(2,1)S(1)}, u32[]{:S(2)}, u32[]{:S(2)}) collective-permute-start(bf16[18,1,16,256]{3,2,1,0:T(8,128)(2,1)S(1)} %get-tuple-element.12), channel_id=1, source_target_pairs={{2,0},{3,1},{6,4},{7,5},{10,8},{11,9},{14,12},{15,13},{18,16},{19,... | collective-permute-start | bytes 442376 | tf_op jit(solution)/shard_map/ppermute | solution.py:20
  53.1 6.3 %collective-permute-start.9 = (bf16[18,1,16,256]{3,2,1,0:T(8,128)(2,1)S(1)}, bf16[18,1,16,256]{3,2,1,0:T(8,128)(2,1)S(1)}, u32[]{:S(2)}, u32[]{:S(2)}) collective-permute-start(bf16[18,1,16,256]{3,2,1,0:T(8,128)(2,1)S(1)} %get-tuple-element.11), channel_id=1, source_target_pairs={{0,2},{1,3},{4,6},{5,7},{8,10},{9,11},{12,14},{13,15},{16,18},{17,... | collective-permute-start | bytes 442376 | tf_op jit(solution)/shard_map/ppermute | solution.py:17
  60.1 5.8 %collective-permute-start.10 = (bf16[18,18,1,256]{3,1,2,0:T(8,128)(2,1)S(1)}, bf16[18,18,1,256]{3,1,2,0:T(8,128)(2,1)S(1)}, u32[]{:S(2)}, u32[]{:S(2)}) collective-permute-start(bf16[18,18,1,256]{3,1,2,0:T(8,128)(2,1)S(1)} %copy.44), channel_id=1, source_target_pairs={{1,0},{3,2},{5,4},{7,6},{9,8},{11,10},{13,12},{15,14},{17,16},{19,... | collective-permute-start | bytes 497672 | tf_op jit(solution)/shard_map/ppermute | solution.py:20
  64.6 3.4 %collective-permute-start.11 = (bf16[18,18,1,256]{3,1,2,0:T(8,128)(2,1)S(1)}, bf16[18,18,1,256]{3,1,2,0:T(8,128)(2,1)S(1)}, u32[]{:S(2)}, u32[]{:S(2)}) collective-permute-start(bf16[18,18,1,256]{3,1,2,0:T(8,128)(2,1)S(1)} %copy.46), channel_id=1, source_target_pairs={{0,1},{2,3},{4,5},{6,7},{8,9},{10,11},{12,13},{14,15},{16,17},{18,... | collective-permute-start | bytes 497672 | tf_op jit(solution)/shard_map/ppermute | solution.py:17
  81.9 1.3 copy-start
Sparse Core Ops, SparseCore 0:
  110.1 92.1 all-reduce.1
where the time goes:
time: 222 us; the launch traced here: 221 us
  waiting for transfers between devices  69.7 us (31%)
  starting transfers between devices  33.6 us (15%)
  other arithmetic  31.8 us (14%)
  blocking collectives  31.3 us (14%)
  local copies, waits for them, and re-layouts  29.1 us (13%)
  between operations  14.7 us (7%)
  matrix products  11.2 us (5%)
    psum x1, waiting for transfers between devices, per_device(): gram_full, coupling = lax.psum((gram_part, couple_part), ('gx', 'gy', 'gz'))  60.8 us
    psum x1, blocking collectives, per_device(): gram_full, coupling = lax.psum((gram_part, couple_part), ('gx', 'gy', 'gz'))  31.3 us
    convert_element_type x2, other arithmetic, advance(): (centre + diffusion * laplace - 0.5 * transport).astype(jnp.bfloat16)  23.6 us
    ppermute x6, starting transfers between devices, padded_2(): lax.ppermute(lax.slice_in_dim(block, block.shape[dim] - width, None, axis...  18.9 us
    ppermute x6, starting transfers between devices, padded_2(): lax.ppermute(lax.slice_in_dim(block, 0, width, axis=dim), axis, backward)  14.7 us
    gather x1, local copies, waits for them, and re-layouts, per_device(): mean_at = jnp.take(mean_flat, obs_spots, axis=0)  11.8 us
    gather x1, local copies, waits for them, and re-layouts, per_device(): picked = jnp.take(flat_anom, obs_spots, axis=0)  9.06 us
    dot_general x16, matrix products, product(): return jnp.dot(left, right, precision=lax.Precision.HIGHEST)  7.69 us
  transfers between devices with their start and end apart: 13, of which 9 were waited for; matrix products, arithmetic and copies ran while one was open for 3% of the time, Pallas kernels for 0%

commit v1 on v0

--- a/solution.py
+++ b/solution.py
@@ -88,7 +88,7 @@
         scaled, scaled, (((0,), (0,)), ((), ())), preferred_element_type=jnp.float32
     )
     couple_part = jnp.dot(innovation, scaled, preferred_element_type=jnp.float32)
-    gram_full, coupling = lax.psum((gram_part, couple_part), ("gx", "gy", "gz"))
+    gram_full, coupling = lax.psum(lax.psum((gram_part, couple_part), ("gy", "gz")), "gx")
     transform = inverse_root(gram_full)
     shift = product(transform, product(transform, coupling))
     weights = (transform + shift[:, None]).astype(jnp.bfloat16)

time: 222 us -> 203 us (0.914)
  blocking collectives: 31.3 us -> 17.1 us
  waiting for transfers between devices: 69.7 us -> 62.7 us
    psum x1 -> x2, blocking collectives: 31.3 us -> 17.1 us  [the longest x1 9.92 us: per_device(): lax.psum(lax.psum((gram_part, couple_part), ('gy', 'gz')), 'gx')]
    psum x1 -> x2, waiting for transfers between devices: 60.8 us -> 53.8 us  [the longest x1 33.2 us: per_device(): lax.psum((gram_part, couple_part), ('gy', 'gz'))]
  transfers between devices with their start and end apart: 13 -> 14, of which waited for: 9 -> 10; matrix products, arithmetic and copies ran while one was open for 3% -> 3% of each run, Pallas kernels for 0% -> 0%
where the time goes in v1:
time: 203 us; the launch traced here: 200 us
  waiting for transfers between devices  62.7 us (31%)
  starting transfers between devices  33.6 us (17%)
  other arithmetic  31.8 us (16%)
  local copies, waits for them, and re-layouts  29.1 us (14%)
  blocking collectives  17.1 us (8%)
  between operations  14.7 us (7%)
  matrix products  11.2 us (6%)
    psum x1, waiting for transfers between devices, per_device(): lax.psum((gram_part, couple_part), ('gy', 'gz'))  33.2 us
    convert_element_type x2, other arithmetic, advance(): (centre + diffusion * laplace - 0.5 * transport).astype(jnp.bfloat16)  23.6 us
    psum x1, waiting for transfers between devices, per_device(): lax.psum(lax.psum((gram_part, couple_part), ('gy', 'gz')), 'gx')  20.6 us
    ppermute x6, starting transfers between devices, padded_2(): lax.ppermute(lax.slice_in_dim(block, block.shape[dim] - width, None, axis...  18.9 us
    ppermute x6, starting transfers between devices, padded_2(): lax.ppermute(lax.slice_in_dim(block, 0, width, axis=dim), axis, backward)  14.7 us
    gather x1, local copies, waits for them, and re-layouts, per_device(): mean_at = jnp.take(mean_flat, obs_spots, axis=0)  11.8 us
    psum x1, blocking collectives, per_device(): lax.psum(lax.psum((gram_part, couple_part), ('gy', 'gz')), 'gx')  9.92 us
    gather x1, local copies, waits for them, and re-layouts, per_device(): picked = jnp.take(flat_anom, obs_spots, axis=0)  9.06 us
  transfers between devices with their start and end apart: 14, of which 10 were waited for; matrix products, arithmetic and copies ran while one was open for 3% of the time, Pallas kernels for 0%

profile of v1, /device:TPU:1, one launch (start us, length us, event | category | flops | bytes accessed | tf_op | source)
XLA Modules:
  0.0 200.2 jit_solution(3066018443840979386)
XLA Ops:
  6.5 1.0 fusion.37
  7.5 4.0 %collective-permute-start.1 = (bf16[1,16,16,256]{3,2,1,0:T(8,128)(2,1)S(1)}, bf16[1,16,16,256]{3,2,1,0:T(8,128)(2,1)S(1)}, u32[]{:S(2)}, u32[]{:S(2)}) collective-permute-start(bf16[1,16,16,256]{3,2,1,0:T(8,128)(2,1)S(1)} %get-tuple-element.18), channel_id=1, source_target_pairs={{0,4},{4,8},{8,12},{1,5},{5,9},{9,13},{2,6},{6,10},{10,14},{3,7},{... | collective-permute-start | bytes 393224 | tf_op jit(solution)/shard_map/ppermute | solution.py:17
  11.6 1.3 collective-permute-start
  12.9 0.8 collective-permute-done.1
  13.7 1.8 constant_dynamic-update-slice_fusion.1
  15.6 1.7 collective-permute-done
  17.3 1.3 collective-permute-start.2
  18.6 4.0 %collective-permute-start.3 = (bf16[18,1,16,256]{3,2,1,0:T(8,128)(2,1)S(1)}, bf16[18,1,16,256]{3,2,1,0:T(8,128)(2,1)S(1)}, u32[]{:S(2)}, u32[]{:S(2)}) collective-permute-start(bf16[18,1,16,256]{3,2,1,0:T(8,128)(2,1)S(1)} %get-tuple-element.13), channel_id=1, source_target_pairs={{0,2},{1,3},{4,6},{5,7},{8,10},{9,11},{12,14},{13,15},{16,18},{17,... | collective-permute-start | bytes 442376 | tf_op jit(solution)/shard_map/ppermute | solution.py:17
  23.2 1.5 collective-permute-done.3
  24.7 0.5 pad_maximum_fusion.35
  25.3 5.2 %collective-permute-start.4 = (bf16[18,18,1,256]{3,1,2,0:T(8,128)(2,1)S(1)}, bf16[18,18,1,256]{3,1,2,0:T(8,128)(2,1)S(1)}, u32[]{:S(2)}, u32[]{:S(2)}) collective-permute-start(bf16[18,18,1,256]{3,1,2,0:T(8,128)(2,1)S(1)} %copy.40), channel_id=1, source_target_pairs={{1,0},{3,2},{5,4},{7,6},{9,8},{11,10},{13,12},{15,14},{17,16},{19,... | collective-permute-start | bytes 497672 | tf_op jit(solution)/shard_map/ppermute | solution.py:20
  30.5 1.4 collective-permute-start.5
  32.0 1.1 slice_bitcast_fusion.2
  33.3 0.7 collective-permute-done.5
  34.3 10.0 %fusion.6 = bf16[16,16,16,256]{3,2,1,0:T(8,128)(2,1)S(1)} fusion(bf16[16,16,16,256]{3,2,1,0:T(8,128)(2,1)S(1)} %copy-done.3, bf16[18,18,1,256]{3,2,1,0:T(2,128)(2,1)S(1)} %copy.43, bf16[18,1,16,256]{3,2,1,0:T(8,128)(2,1)S(1)} %collective-permute-done.2, bf16[18,16,16,256]{3,2,1,0:T(8,128)(2,1)S(1)} %copy-done.2, ...), kind=kLoop, calls=%fused_computation.33 | loop fusion | flops 57671680 | bytes 7491584 | tf_op jit(solution)/shard_map/convert_element_type | solution.py:38
  44.3 1.3 collective-permute-start.6
  45.6 4.0 %collective-permute-start.7 = (bf16[1,16,16,256]{3,2,1,0:T(8,128)(2,1)S(1)}, bf16[1,16,16,256]{3,2,1,0:T(8,128)(2,1)S(1)}, u32[]{:S(2)}, u32[]{:S(2)}) collective-permute-start(bf16[1,16,16,256]{3,2,1,0:T(8,128)(2,1)S(1)} %get-tuple-element.15), channel_id=1, source_target_pairs={{0,4},{4,8},{8,12},{1,5},{5,9},{9,13},{2,6},{6,10},{10,14},{3,7},{... | collective-permute-start | bytes 393224 | tf_op jit(solution)/shard_map/ppermute | solution.py:17
  49.7 1.1 collective-permute-done.6
  50.9 0.9 collective-permute-done.7
  51.8 1.3 collective-permute-start.8
  53.1 4.1 %collective-permute-start.9 = (bf16[18,1,16,256]{3,2,1,0:T(8,128)(2,1)S(1)}, bf16[18,1,16,256]{3,2,1,0:T(8,128)(2,1)S(1)}, u32[]{:S(2)}, u32[]{:S(2)}) collective-permute-start(bf16[18,1,16,256]{3,2,1,0:T(8,128)(2,1)S(1)} %get-tuple-element.11), channel_id=1, source_target_pairs={{0,2},{1,3},{4,6},{5,7},{8,10},{9,11},{12,14},{13,15},{16,18},{17,... | collective-permute-start | bytes 442376 | tf_op jit(solution)/shard_map/ppermute | solution.py:17
  57.2 0.9 convert_multiply_fusion.4
  58.3 0.9 copy.54
  59.3 0.7 pad_maximum_fusion.32
  60.1 4.4 %collective-permute-start.10 = (bf16[18,18,1,256]{3,1,2,0:T(8,128)(2,1)S(1)}, bf16[18,18,1,256]{3,1,2,0:T(8,128)(2,1)S(1)}, u32[]{:S(2)}, u32[]{:S(2)}) collective-permute-start(bf16[18,18,1,256]{3,1,2,0:T(8,128)(2,1)S(1)} %copy.44), channel_id=1, source_target_pairs={{1,0},{3,2},{5,4},{7,6},{9,8},{11,10},{13,12},{15,14},{17,16},{19,... | collective-permute-start | bytes 497672 | tf_op jit(solution)/shard_map/ppermute | solution.py:20
  64.6 1.3 collective-permute-start.11
  66.2 1.8 collective-permute-done.11
  68.2 13.7 %fusion.16 = bf16[16,16,16,256]{3,2,1,0:T(8,128)(2,1)S(1)} fusion(bf16[16,16,16,256]{3,2,1,0:T(8,128)(2,1)S(1)} %fusion.6, bf16[18,18,1,256]{3,2,1,0:T(2,128)(2,1)S(1)} %copy.47, bf16[18,1,16,256]{3,2,1,0:T(8,128)(2,1)S(1)} %collective-permute-done.8, bf16[18,1,16,256]{3,2,1,0:T(8,128)(2,1)S(1)} %collective-permute-done.9, ...), kind=kLoop, calls=%fused_computation.43 | loop fusion | flops 74448896 | bytes 5132288 | tf_op jit(solution)/shard_map/convert_element_type | solution.py:38
  81.9 1.3 copy-done
  83.2 0.6 convert_reduce_fusion
  84.0 1.9 fusion.21
  86.1 9.1 %gather_fusion = bf16[2048,256]{1,0:T(8,128)(2,1)} fusion(bf16[4096,256]{1,0:T(8,128)(2,1)S(1)} %bitcast.48, s32[2048]{0:T(1024)S(1)} %broadcast_clamp_fusion), kind=kCustom, calls=%fused_computation | custom fusion | bytes 2105344 | tf_op jit(solution)/shard_map/jit(_take)/gather | solution.py:75
  95.2 11.8 %gather_fusion.1 = f32[2048]{0:T(1024)S(1)} fusion(f32[4096]{0:T(1024)S(1)} %div.28, s32[2048]{0:T(1024)S(1)} %broadcast_clamp_fusion), kind=kCustom, calls=%fused_computation.1 | custom fusion | bytes 24576 | tf_op jit(solution)/shard_map/jit(_take)/gather | solution.py:76
  107.0 1.8 multiply_convert_fusion
  108.7 1.2 fusion.38
  110.0 33.2 %all-reduce.3.cloned.1.call-done = f32[256,256]{1,0:T(8,128)} async-done(((f32[256,256]{1,0:T(8,128)}), f32[256,256]{1,0:T(8,128)}) %all-reduce.3.cloned.1.call-update) | async-done | bytes 262160 | tf_op jit(solution)/shard_map/psum | solution.py:91
  143.4 7.2 %psum.30 = f32[256]{0:T(256)S(1)} all-reduce(f32[256]{0:T(256)S(1)} %bitcast.53), channel_id=1, replica_groups=mesh['grp'=2,'gx'=4,'gy'=2,'gz'=2] {'gy','gz'}, use_global_device_ids=true, to_apply=%region_4.5 | all-reduce | flops 256 | bytes 2048 | tf_op jit(solution)/shard_map/psum | solution.py:91
  150.6 9.9 %psum.31 = f32[256]{0:T(256)S(1)} all-reduce(f32[256]{0:T(256)S(1)} %psum.30), channel_id=1, replica_groups=mesh['grp'=2,'gx'=4,'gy'=2,'gz'=2] {'gx'}, use_global_device_ids=true, to_apply=%region_5.6 | all-reduce | flops 256 | bytes 2048 | tf_op jit(solution)/shard_map/psum | solution.py:91
  160.5 20.6 %all-reduce.5.cloned.1.call-done = f32[256,256]{1,0:T(8,128)} async-done(((f32[256,256]{1,0:T(8,128)}), f32[256,256]{1,0:T(8,128)}) %all-reduce.5.cloned.1.call-update) | async-done | bytes 262160 | tf_op jit(solution)/shard_map/psum | solution.py:91
  181.1 1.6 multiply_reduce_fusion
  183.4 1.3 fusion.28
  185.0 1.4 fusion.32
  186.4 0.4 fusion.27
  187.5 0.4 fusion.26
  188.7 0.4 fusion.25
  189.9 0.4 fusion.24
  190.3 0.4 convolution_divide_fusion
  191.3 2.1 %fusion = bf16[4096,256]{1,0:T(8,128)(2,1)} fusion(bf16[4096,256]{1,0:T(8,128)(2,1)S(1)} %bitcast.49, f32[4096]{0:T(1024)S(1)} %div.28, f32[256,256]{1,0:T(8,128)S(1)} %convolution_divide_fusion, f32[256]{0:T(256)S(1)} %bitcast.51), kind=kOutput, calls=%fused_computation.27 | convolution fusion | flops 539099136 | bytes 4473856 | tf_op jit(solution)/shard_map/dot_general | solution.py:95
  (55 shorter events, 6.0 us)
Async XLA Ops:
  6.5 136.6 %all-reduce.3.cloned.1.call-start = ((), (), s32[]{:S(2)}) async-start(), calls=%async_computation | async-start | bytes 524288 | tf_op jit(solution)/shard_map/psum | solution.py:91
  7.5 6.2 %collective-permute-start.1 = (bf16[1,16,16,256]{3,2,1,0:T(8,128)(2,1)S(1)}, bf16[1,16,16,256]{3,2,1,0:T(8,128)(2,1)S(1)}, u32[]{:S(2)}, u32[]{:S(2)}) collective-permute-start(bf16[1,16,16,256]{3,2,1,0:T(8,128)(2,1)S(1)} %get-tuple-element.18), channel_id=1, source_target_pairs={{0,4},{4,8},{8,12},{1,5},{5,9},{9,13},{2,6},{6,10},{10,14},{3,7},{... | collective-permute-start | bytes 393224 | tf_op jit(solution)/shard_map/ppermute | solution.py:17
  11.6 5.7 %collective-permute-start = (bf16[1,16,16,256]{3,2,1,0:T(8,128)(2,1)S(1)}, bf16[1,16,16,256]{3,2,1,0:T(8,128)(2,1)S(1)}, u32[]{:S(2)}, u32[]{:S(2)}) collective-permute-start(bf16[1,16,16,256]{3,2,1,0:T(8,128)(2,1)S(1)} %get-tuple-element.17), channel_id=1, source_target_pairs={{4,0},{8,4},{12,8},{5,1},{9,5},{13,9},{6,2},{10,6},{14,10},{7,3},{... | collective-permute-start | bytes 393224 | tf_op jit(solution)/shard_map/ppermute | solution.py:20
  13.7 8.9 %copy-start.4 = (s32[16,16,8]{1,2,0:T(8,128)S(1)}, s32[16,16,8]{1,2,0:T(8,128)}, u32[]{:S(2)}) copy-start(s32[16,16,8]{1,2,0:T(8,128)} %param.10) | copy-start | bytes 24580
  17.3 8.0 %copy-start.1 = (bf16[18,16,16,256]{3,2,1,0:T(8,128)(2,1)}, bf16[18,16,16,256]{3,2,1,0:T(8,128)(2,1)S(1)}, u32[]{:S(2)}) copy-start(bf16[18,16,16,256]{3,2,1,0:T(8,128)(2,1)S(1)} %constant_dynamic-update-slice_fusion) | copy-start | bytes 7077892
  17.3 5.9 %collective-permute-start.2 = (bf16[18,1,16,256]{3,2,1,0:T(8,128)(2,1)S(1)}, bf16[18,1,16,256]{3,2,1,0:T(8,128)(2,1)S(1)}, u32[]{:S(2)}, u32[]{:S(2)}) collective-permute-start(bf16[18,1,16,256]{3,2,1,0:T(8,128)(2,1)S(1)} %get-tuple-element.14), channel_id=1, source_target_pairs={{2,0},{3,1},{6,4},{7,5},{10,8},{11,9},{14,12},{15,13},{18,16},{19,... | collective-permute-start | bytes 442376 | tf_op jit(solution)/shard_map/ppermute | solution.py:20
  18.6 6.1 %collective-permute-start.3 = (bf16[18,1,16,256]{3,2,1,0:T(8,128)(2,1)S(1)}, bf16[18,1,16,256]{3,2,1,0:T(8,128)(2,1)S(1)}, u32[]{:S(2)}, u32[]{:S(2)}) collective-permute-start(bf16[18,1,16,256]{3,2,1,0:T(8,128)(2,1)S(1)} %get-tuple-element.13), channel_id=1, source_target_pairs={{0,2},{1,3},{4,6},{5,7},{8,10},{9,11},{12,14},{13,15},{16,18},{17,... | collective-permute-start | bytes 442376 | tf_op jit(solution)/shard_map/ppermute | solution.py:17
  22.9 11.4 %copy-start.3 = (bf16[16,16,16,256]{3,2,1,0:T(8,128)(2,1)S(1)}, bf16[16,16,16,256]{3,2,1,0:T(8,128)(2,1)}, u32[]{:S(2)}) copy-start(bf16[16,16,16,256]{3,2,1,0:T(8,128)(2,1)} %param.6) | copy-start | bytes 6291460
  25.3 7.7 %collective-permute-start.4 = (bf16[18,18,1,256]{3,1,2,0:T(8,128)(2,1)S(1)}, bf16[18,18,1,256]{3,1,2,0:T(8,128)(2,1)S(1)}, u32[]{:S(2)}, u32[]{:S(2)}) collective-permute-start(bf16[18,18,1,256]{3,1,2,0:T(8,128)(2,1)S(1)} %copy.40), channel_id=1, source_target_pairs={{1,0},{3,2},{5,4},{7,6},{9,8},{11,10},{13,12},{15,14},{17,16},{19,... | collective-permute-start | bytes 497672 | tf_op jit(solution)/shard_map/ppermute | solution.py:20
  30.5 3.8 %copy-start.2 = (bf16[18,16,16,256]{3,2,1,0:T(8,128)(2,1)S(1)}, bf16[18,16,16,256]{3,2,1,0:T(8,128)(2,1)}, u32[]{:S(2)}) copy-start(bf16[18,16,16,256]{3,2,1,0:T(8,128)(2,1)} %copy-done.1) | copy-start | bytes 7077892
  30.5 3.5 %collective-permute-start.5 = (bf16[18,18,1,256]{3,1,2,0:T(8,128)(2,1)S(1)}, bf16[18,18,1,256]{3,1,2,0:T(8,128)(2,1)S(1)}, u32[]{:S(2)}, u32[]{:S(2)}) collective-permute-start(bf16[18,18,1,256]{3,1,2,0:T(8,128)(2,1)S(1)} %copy.42), channel_id=1, source_target_pairs={{0,1},{2,3},{4,5},{6,7},{8,9},{10,11},{12,13},{14,15},{16,17},{18,... | collective-permute-start | bytes 497672 | tf_op jit(solution)/shard_map/ppermute | solution.py:17
  44.3 6.5 %collective-permute-start.6 = (bf16[1,16,16,256]{3,2,1,0:T(8,128)(2,1)S(1)}, bf16[1,16,16,256]{3,2,1,0:T(8,128)(2,1)S(1)}, u32[]{:S(2)}, u32[]{:S(2)}) collective-permute-start(bf16[1,16,16,256]{3,2,1,0:T(8,128)(2,1)S(1)} %get-tuple-element.16), channel_id=1, source_target_pairs={{4,0},{8,4},{12,8},{5,1},{9,5},{13,9},{6,2},{10,6},{14,10},{7,3},{... | collective-permute-start | bytes 393224 | tf_op jit(solution)/shard_map/ppermute | solution.py:20
  45.6 6.1 %collective-permute-start.7 = (bf16[1,16,16,256]{3,2,1,0:T(8,128)(2,1)S(1)}, bf16[1,16,16,256]{3,2,1,0:T(8,128)(2,1)S(1)}, u32[]{:S(2)}, u32[]{:S(2)}) collective-permute-start(bf16[1,16,16,256]{3,2,1,0:T(8,128)(2,1)S(1)} %get-tuple-element.15), channel_id=1, source_target_pairs={{0,4},{4,8},{8,12},{1,5},{5,9},{9,13},{2,6},{6,10},{10,14},{3,7},{... | collective-permute-start | bytes 393224 | tf_op jit(solution)/shard_map/ppermute | solution.py:17
  51.8 7.6 %collective-permute-start.8 = (bf16[18,1,16,256]{3,2,1,0:T(8,128)(2,1)S(1)}, bf16[18,1,16,256]{3,2,1,0:T(8,128)(2,1)S(1)}, u32[]{:S(2)}, u32[]{:S(2)}) collective-permute-start(bf16[18,1,16,256]{3,2,1,0:T(8,128)(2,1)S(1)} %get-tuple-element.12), channel_id=1, source_target_pairs={{2,0},{3,1},{6,4},{7,5},{10,8},{11,9},{14,12},{15,13},{18,16},{19,... | collective-permute-start | bytes 442376 | tf_op jit(solution)/shard_map/ppermute | solution.py:20
  53.1 6.3 %collective-permute-start.9 = (bf16[18,1,16,256]{3,2,1,0:T(8,128)(2,1)S(1)}, bf16[18,1,16,256]{3,2,1,0:T(8,128)(2,1)S(1)}, u32[]{:S(2)}, u32[]{:S(2)}) collective-permute-start(bf16[18,1,16,256]{3,2,1,0:T(8,128)(2,1)S(1)} %get-tuple-element.11), channel_id=1, source_target_pairs={{0,2},{1,3},{4,6},{5,7},{8,10},{9,11},{12,14},{13,15},{16,18},{17,... | collective-permute-start | bytes 442376 | tf_op jit(solution)/shard_map/ppermute | solution.py:17
  60.1 5.8 %collective-permute-start.10 = (bf16[18,18,1,256]{3,1,2,0:T(8,128)(2,1)S(1)}, bf16[18,18,1,256]{3,1,2,0:T(8,128)(2,1)S(1)}, u32[]{:S(2)}, u32[]{:S(2)}) collective-permute-start(bf16[18,18,1,256]{3,1,2,0:T(8,128)(2,1)S(1)} %copy.44), channel_id=1, source_target_pairs={{1,0},{3,2},{5,4},{7,6},{9,8},{11,10},{13,12},{15,14},{17,16},{19,... | collective-permute-start | bytes 497672 | tf_op jit(solution)/shard_map/ppermute | solution.py:20
  64.6 3.4 %collective-permute-start.11 = (bf16[18,18,1,256]{3,1,2,0:T(8,128)(2,1)S(1)}, bf16[18,18,1,256]{3,1,2,0:T(8,128)(2,1)S(1)}, u32[]{:S(2)}, u32[]{:S(2)}) collective-permute-start(bf16[18,18,1,256]{3,1,2,0:T(8,128)(2,1)S(1)} %copy.46), channel_id=1, source_target_pairs={{0,1},{2,3},{4,5},{6,7},{8,9},{10,11},{12,13},{14,15},{16,17},{18,... | collective-permute-start | bytes 497672 | tf_op jit(solution)/shard_map/ppermute | solution.py:17
  81.9 1.3 copy-start
  109.9 71.2 %all-reduce.5.cloned.1.call-start = ((), (), s32[]{:S(2)}) async-start(), calls=%async_computation.1 | async-start | bytes 524288 | tf_op jit(solution)/shard_map/psum | solution.py:91
Sparse Core Ops, SparseCore 0:
  110.0 33.0 all-reduce.2
  145.6 35.4 all-reduce.4
